TPU v7x, 512 devices: a whole 4x8x8 slice. The times are simulated.
512 devices in a mesh: dp: 64 (over y_lo, z, core), mp: 8 (over y_hi, x).
Axes of the slice: x: 4, y: 8 (y_hi: 2, y_lo: 4; y = y_hi * 4 + y_lo), z: 8, core: 2. Of those that a mesh axis runs over, the one named last changes fastest.
Arguments:
- tokens: bfloat16 [3072, 16384], P('dp', 'mp'), may hold values from -6 to 6
- codes: int32 [16384, 8192], P('mp', 'dp'), may hold values from -8 to 7
- expo: int32 [128, 8192], P('mp', 'dp'), may hold values from -4 to -1
- rounding: float32 [16384, 8192], P('mp', 'dp'), may hold values from -6 to 6
- target: bfloat16 [3072, 8192], P(None, 'dp'), may hold values from -32 to 32
Outputs:
- new_rounding: float32 [16384, 8192], P('mp', 'dp')
- loss: float32 [], replicated
All inputs are finite; a program needn't handle non-finite values.
Results may differ from a plain program's by a relative error of at most 0.0004.
The roundings to bfloat16 on the way count: a program that leaves them out, or rounds other values in their place, can miss the bound.
Values may be sent and summed in bfloat16 or wider, within the bound.
A program may use at most 64 MiB of HBM per device.

v0:
```python
import jax
import jax.numpy as jnp
from jax import lax
from jax.sharding import PartitionSpec as P

D = 16384
FW = 8192
GROUP = 128


STRETCH_HIGH = 1.1
STRETCH_LOW = -0.1
LIMIT = 2.3978952727983707
REG_WEIGHT = 0.01
STEP_SIZE = 0.5
EPSILON = 1e-06


def soft_round(rounding):
    sigma = jax.nn.sigmoid(rounding)
    soft = jnp.clip(sigma * (STRETCH_HIGH - STRETCH_LOW) + STRETCH_LOW, 0.0, 1.0)
    slope = jnp.where(
        jnp.abs(rounding) < LIMIT, (STRETCH_HIGH - STRETCH_LOW) * sigma * (1.0 - sigma), 0.0
    )
    return (soft, slope)


def group_scale(expo):
    return jnp.repeat(jnp.exp2(expo.astype(jnp.float32)) * D ** (-0.5), GROUP, axis=0)


def local(tokens, codes, expo, rounding, target):
    model_count = lax.axis_size("mp")
    numel = float(D * FW)
    soft, slope = soft_round(rounding)
    scale = group_scale(expo)
    weights = (scale * (codes.astype(jnp.float32) + soft)).astype(jnp.bfloat16)
    target_f = target.astype(jnp.float32)
    local_energy = jnp.sum(target_f * target_f)
    energy = lax.psum(local_energy, "dp")
    gathered = lax.all_gather(tokens, "dp", axis=0, tiled=True)
    partial_pre = jnp.dot(gathered, weights, preferred_element_type=jnp.float32)
    pre = lax.psum(partial_pre, "mp")
    share = 1.0 / model_count
    sigma_pre = jax.nn.sigmoid(pre)
    diff = pre * sigma_pre - target_f
    upstream = (2.0 * diff * sigma_pre * (1.0 + pre * (1.0 - sigma_pre))).astype(jnp.bfloat16)
    error_sum = jnp.sum(diff * diff) * share
    wgrad = lax.dot_general(
        gathered, upstream, (((0,), (0,)), ((), ())), preferred_element_type=jnp.float32
    )
    centered = 2.0 * soft - 1.0
    direct = scale * slope * wgrad
    reg_term = -REG_WEIGHT * 8.0 * centered * centered * centered * slope
    regular = jnp.sum(1.0 - centered * centered * centered * centered)
    factor = numel / energy
    grad = factor * direct + reg_term
    grad_sq, error_total, reg_total = lax.psum(
        (jnp.sum(grad * grad), error_sum, regular), ("dp", "mp")
    )
    rms = jnp.sqrt(grad_sq / numel + EPSILON)
    new_rounding = rounding - STEP_SIZE * grad / rms
    loss = error_total / energy + REG_WEIGHT * reg_total / numel
    return (new_rounding, loss)


def solution(mesh):
    in_specs = (P("dp", "mp"), P("mp", "dp"), P("mp", "dp"), P("mp", "dp"), P(None, "dp"))
    out_specs = (P("mp", "dp"), P())
    return jax.shard_map(local, mesh=mesh, in_specs=in_specs, out_specs=out_specs, check_vma=False)
```

profile of v0, /device:TPU:1, one launch (start us, length us, event | category | flops | bytes accessed | tf_op | source)
XLA Modules:
  0.0 541.2 jit_solution(11852524219915668825)
XLA Ops:
  7.2 0.0 copy-start.4
  7.2 0.0 copy-start.1
  7.2 0.0 all-gather.2.cloned.1.call-start
  7.2 0.7 all-gather.2.cloned.1.call-update
  7.9 0.0 all-reduce.3.cloned.1.call-start
  8.0 1.6 copy.12
  9.6 0.1 copy.8
  9.7 0.0 copy-done.1
  9.7 0.3 copy.11
  10.0 136.2 %all-gather.2.cloned.1.call-done = bf16[3072,2048]{1,0:T(8,128)(2,1)} async-done(((bf16[48,2048]{1,0:T(8,128)(2,1)}), bf16[3072,2048]{1,0:T(8,128)(2,1)}) %all-gather.2.cloned.1.call-update) | async-done | bytes 12582928 | tf_op jit(solution)/shard_map/all_gather | solution.py:41
  146.2 0.3 broadcast_in_dim.7
  146.5 1.0 copy-done.2
  147.5 10.0 %convolution_bitcast_fusion = f32[3072,128]{0,1:T(8,128)} fusion(bf16[3072,2048]{1,0:T(8,128)(2,1)} %all-gather.2.cloned.1.call-done, s32[2048,128]{0,1:T(8,128)S(1)} %copy.11, f32[16,8,16,128]{3,2,1,0:T(8,128)S(1)} %bitcast.23, f32[2048,128]{0,1:T(8,128)S(1)} %copy.12), kind=kOutput, calls=%fused_computation | convolution fusion | flops 1613234176 | bytes 17301504 | tf_op jit(solution)/shard_map/dot_general | solution.py:42
  157.5 0.0 all-reduce.3.cloned.1.call-update
  157.6 1.1 copy-done.3
  158.7 0.3 copy.7
  159.0 1.1 fusion.6
  160.1 122.1 %all-reduce.3.cloned.1.call-done = f32[3072,128]{0,1:T(8,128)} async-done(((f32[3072,128]{0,1:T(8,128)}), f32[3072,128]{0,1:T(8,128)}) %all-reduce.3.cloned.1.call-update) | async-done | bytes 1572880 | tf_op jit(solution)/shard_map/psum | solution.py:43
  282.2 2.8 multiply_reduce_fusion
  285.0 135.6 %psum.35 = f32[]{:T(128)} all-reduce(f32[]{:T(128)} %get-tuple-element.5), channel_id=1, replica_groups=mesh['dp'=64,'mp'=8] {'dp'}, use_global_device_ids=true, to_apply=%region_1.2 | all-reduce | flops 1 | bytes 8 | tf_op jit(solution)/shard_map/psum | solution.py:40
  422.0 9.7 %multiply_reduce_fusion.1 = (f32[]{:T(128)}, f32[2048,128]{0,1:T(8,128)}) fusion(bf16[3072,2048]{1,0:T(8,128)(2,1)} %all-gather.2.cloned.1.call-done, f32[3072,128]{0,1:T(8,128)S(1)} %copy-done, bf16[3072,128]{0,1:T(8,128)(2,1)S(1)} %copy.7, f32[2048,128]{0,1:T(8,128)S(1)} %copy.12, f32[16,8,16,128]{3,2,1,0:T(8,128)} %bitcast.24, f32[]{:T(128)S(6)} %div.24), kind=kOutput, calls=%fused_computation.20 | convolution fusion | flops 1621753856 | bytes 18087944 | tf_op jit(solution)/shard_map/dot_general | solution.py:49
  431.7 96.2 %all-reduce = (f32[]{:T(128)}, f32[]{:T(128)}, f32[]{:T(128)}) all-reduce(f32[]{:T(128)} %get-tuple-element.9, f32[]{:T(128)S(6)} %mul.121, f32[]{:T(128)} %fusion.6), channel_id=1, replica_groups=mesh['dp'=64,'mp'=8] {'dp','mp'}, use_global_device_ids=true, to_apply=%region_4.5 | all-reduce | flops 3 | bytes 24 | tf_op jit(solution)/shard_map/psum | solution.py:58
  529.9 1.3 divide_subtract_fusion
  531.3 1.3 copy.13
  (6 shorter events, 0.0 us)
Async XLA Ops:
  7.2 2.4 copy-start.4
  7.2 2.5 copy-start.1
  7.2 139.0 %all-gather.2.cloned.1.call-start = ((), (), s32[]{:S(2)}) async-start(), calls=%async_computation | async-start | bytes 12779520 | tf_op jit(solution)/shard_map/all_gather | solution.py:41
  7.9 274.3 %all-reduce.3.cloned.1.call-start = ((), (), s32[]{:S(2)}) async-start(), calls=%async_computation.1 | async-start | bytes 3145728 | tf_op jit(solution)/shard_map/psum | solution.py:43
  146.5 1.0 copy-start.2
  157.5 1.1 copy-start.3
  282.2 139.7 %copy-start = (f32[3072,128]{0,1:T(8,128)S(1)}, f32[3072,128]{0,1:T(8,128)}, u32[]{:S(2)}) copy-start(f32[3072,128]{0,1:T(8,128)} %all-reduce.3.cloned.1.call-done) | copy-start | bytes 4718596
Sparse Core Ops, SparseCore 0:
  10.2 135.9 all-gather.1
  157.7 124.4 all-reduce.2
where the time goes:
time: 542 us; the launch traced here: 541 us
  waiting for transfers between devices  259 us (48%)
  blocking collectives  232 us (43%)
  matrix products  19.7 us (4%)
  between operations  19.2 us (4%)
  local copies, waits for them, and re-layouts  5.99 us (1%)
    all_gather x1, waiting for transfers between devices, local(): gathered = lax.all_gather(tokens, 'dp', axis=0, tiled=True)  136 us
    psum x1, blocking collectives, local(): energy = lax.psum(local_energy, 'dp')  136 us
    psum x1, waiting for transfers between devices, local(): pre = lax.psum(partial_pre, 'mp')  122 us
    psum x1, blocking collectives, local(): lax.psum((jnp.sum(grad * grad), error_sum, regular), ('dp', 'mp'))  96.2 us
  transfers between devices with their start and end apart: 2, of which 2 were waited for; matrix products, arithmetic and copies ran while one was open for 1% of the time, Pallas kernels for 0%

commit v1 on v0

v1 whole, which is shorter than its diff:
```python
import functools

import jax
import jax.numpy as jnp
from jax import lax
from jax.experimental import pallas as pl
from jax.experimental.pallas import tpu as pltpu
from jax.sharding import PartitionSpec as P

D = 16384
FW = 8192
GROUP = 128
STRETCH_HIGH = 1.1
STRETCH_LOW = -0.1
LIMIT = 2.3978952727983707
REG_WEIGHT = 0.01
STEP_SIZE = 0.5
EPSILON = 1e-06

NX, NYL, NYH, NZ, NC = 4, 4, 2, 8, 2
NQ = NX * NC
NY = NYL * NYH
MESH = pl.DeviceIdType.MESH
F32 = jnp.float32
BF16 = jnp.bfloat16


def rem(a, n):
    return lax.rem(a, jnp.int32(n))


def div(a, n):
    return lax.div(a, jnp.int32(n))


def aligned(a, n):
    return pl.ds(pl.multiple_of(a * n, n), n)


def kernel(
    tokens, codes, expo, rounding, target, out, loss,
    xs, codes_v, expo_v, round_v, tgt, scale_v, ss, reg, grad, w_full, w, part, rbuf, r2, r3, up, gacc, grecv,
    err, red_src, red_buf, energy_v,
    in_sem, tgt_sem, loc_sem, wl_sem, out_sem,
    ys, yr, zs, zr, ws, wr, s1s, s1r, s2s, s2r, s3s, s3r, s4s, s4r, gs, gr, rs, rr,
):
    dp, mp = lax.axis_index("dp"), lax.axis_index("mp")
    core = rem(dp, NC)
    z = rem(div(dp, NC), NZ)
    yl = div(dp, NC * NZ)
    x = rem(mp, NX)
    yh = div(mp, NX)
    q = x * NC + core
    y = yh * NYL + yl

    def dev(x_, yh_, yl_, z_, c_):
        return ((yl_ * NZ + z_) * NC + c_, yh_ * NX + x_)

    rows, kd = tokens.shape
    kh = kd // NC
    blk = rows * NC
    half = blk // NYH
    cols = codes.shape[1]
    groups = kh // GROUP

    def q_dev(o):
        t = rem(q + o, NQ)
        return div(t, NC), rem(t, NC)

    def y_dev(o):
        t = rem(y + o, NY)
        return dev(x, div(t, NYL), rem(t, NYL), z, core)

    def z_dev(o):
        return dev(x, yh, yl, rem(z + o, NZ), core)

    z_up, z_down = z_dev(1), z_dev(NZ - 1)
    sib = dev(x, yh, yl, z, 1 - core)
    y_peer = dev(x, 1 - yh, yl, z, core)

    def copy(src, dst, ssem, rsem, to):
        return pltpu.make_async_remote_copy(
            src_ref=src, dst_ref=dst, send_sem=ssem, recv_sem=rsem, device_id=to, device_id_type=MESH
        )

    loads = [
        pltpu.make_async_copy(rounding, round_v, in_sem.at[0]),
        pltpu.make_async_copy(codes, codes_v, in_sem.at[1]),
        pltpu.make_async_copy(expo, expo_v, in_sem.at[2]),
    ]
    for load in loads:
        load.start()
    for s in range(NZ):
        at = pl.multiple_of(x * (NZ * blk) + s * blk + yh * half, 16)
        pltpu.make_async_copy(target.at[pl.ds(at, half)], tgt.at[s], tgt_sem).start()

    barrier = pltpu.get_barrier_semaphore()
    partners = []
    for o in range(1, NQ):
        x_, c_ = q_dev(o)
        partners.append(dev(x_, yh, yl, z, c_))
    for o in range(1, NY):
        partners.append(y_dev(o))
    for o in range(1, NZ):
        partners.append(z_dev(o))
    for j in range(1, NYL):
        partners.append(dev(x, yh, rem(yl + j, NYL), z, 1 - core))
    for partner in partners:
        pl.semaphore_signal(barrier, inc=1, device_id=partner, device_id_type=MESH)
    pl.semaphore_wait(barrier, len(partners))

    def own_rows(y_, c_):
        return pl.ds(pl.multiple_of(y_ * blk + c_ * rows, 16), rows)

    def token_half(h):
        return tokens.at[:, pl.ds(pl.multiple_of(h * kh, 128), kh)]

    mine = own_rows(yl, core)
    local = pltpu.make_async_copy(token_half(core), xs.at[z, mine], loc_sem)
    local.start()
    copy(token_half(1 - core), xs.at[z, mine], ys, yr.at[yl, core], sib).start()
    for j in range(1, NYL):
        for h in range(NC):
            copy(token_half(h), xs.at[z, mine], ys, yr.at[yl, core], dev(x, yh, rem(yl + j, NYL), z, h)).start()

    def piece(s, y_):
        return xs.at[s, aligned(y_, blk)]

    def forward(s, y_, d, up_flow):
        k, to = (0, z_up) if up_flow else (1, z_down)
        copy(piece(s, y_), piece(s, y_), zs.at[k, d], zr.at[s, y_], to).start()

    def wait_piece(s, y_):
        copy(piece(s, y_), piece(s, y_), zs.at[0, 0], zr.at[s, y_], z_up).wait_recv()

    def down_slab(d):
        return rem(z + NZ - d, NZ)

    def up_slab(d):
        return rem(z + d, NZ)

    def red_send(i, st, value):
        red_src[i, st] = value
        for o in range(1, (NQ, NY, NZ)[st]):
            if st == 0:
                x_, c_ = q_dev(o)
                to = dev(x_, yh, yl, z, c_)
            else:
                to = (y_dev, z_dev)[st - 1](o)
            copy(red_src.at[i, st], red_buf.at[i, st, o - 1], rs.at[i, st], rr.at[i, st], to).start()

    def red_recv(i, st):
        n = (NQ, NY, NZ)[st] - 1
        got = red_buf.at[i, st, pl.ds(0, n)]
        copy(got, got, rs.at[i, st], rr.at[i, st], sib).wait_recv()
        total = red_src[i, st]
        for o in range(n):
            total += red_buf[i, st, o]
        return total

    def red_done(i, st):
        n = (NQ, NY, NZ)[st] - 1
        got = red_buf.at[i, st, pl.ds(0, n)]
        copy(got, got, rs.at[i, st], rr.at[i, st], sib).wait_send()

    def fold(a):
        return a.reshape(a.shape[0] // 8, 8, a.shape[1]).sum(axis=0)

    for load in loads:
        load.wait()
    scale_v[...] = jnp.exp2(expo_v[...].astype(F32)) * D ** (-0.5)

    def group_weights(g, total):
        at = aligned(g, GROUP)
        r = round_v[at]
        sigma = jax.nn.sigmoid(r)
        soft = jnp.clip(sigma * (STRETCH_HIGH - STRETCH_LOW) + STRETCH_LOW, 0.0, 1.0)
        slope = jnp.where(jnp.abs(r) < LIMIT, (STRETCH_HIGH - STRETCH_LOW) * sigma * (1.0 - sigma), 0.0)
        scale = scale_v[pl.ds(g, 1)]
        w_full[at] = (scale * (codes_v[at].astype(F32) + soft)).astype(BF16)
        centered = 2.0 * soft - 1.0
        cube = centered * centered * centered
        ss[at] = scale * slope
        reg[at] = -REG_WEIGHT * 8.0 * cube * slope
        return total + fold(1.0 - cube * centered)

    def half_rows(h):
        return aligned(h, kh)

    def weights(h, total):
        return lax.fori_loop(h * groups, (h + 1) * groups, group_weights, total)

    w_cols = w.at[:, aligned(core, cols)]
    regular = weights(1 - core, jnp.zeros((8, cols), F32))
    send_w = copy(w_full.at[half_rows(1 - core)], w_cols, ws, wr, sib)
    send_w.start()
    regular = weights(core, regular)
    local_w = pltpu.make_async_copy(w_full.at[half_rows(core)], w_cols, wl_sem)
    local_w.start()

    pltpu.make_async_copy(tgt, tgt, tgt_sem).wait()
    err[...] = jnp.zeros_like(err)
    energy = jnp.zeros((8, cols), F32)
    for s in range(NZ):
        t = tgt[s].astype(F32)
        energy += fold(t * t)
    red_send(0, 0, energy)
    gacc[...] = jnp.zeros_like(gacc)

    def s1(s):
        def rows_of(j, carry):
            at = aligned(j, blk)
            part[s, at] = jnp.dot(xs[s, at], w[...], preferred_element_type=F32)
            return carry

        lax.fori_loop(0, NYL, rows_of, 0)
        for o in range(1, NQ):
            x_, c_ = q_dev(o)
            copy(
                part.at[s, aligned(x_, blk), aligned(c_, cols)], rbuf.at[s, o - 1], s1s.at[s], s1r.at[s],
                dev(x_, yh, yl, z, c_),
            ).start()

    def s2(s):
        copy(rbuf.at[s], rbuf.at[s], s1s.at[s], s1r.at[s], sib).wait_recv()
        total = part[s, aligned(x, blk), aligned(core, cols)]
        for o in range(NQ - 1):
            total += rbuf[s, o]
        for i in range(NYH):
            r2[s, i] = total[i * half : (i + 1) * half]
        copy(r2.at[s, 1 - yh], r3.at[s], s2s.at[s], s2r.at[s], y_peer).start()

    def up_at(s):
        return up.at[s, pl.ds(pl.multiple_of(x * blk + yh * half, 16), half), aligned(core, cols)]

    def s3(s):
        copy(r3.at[s], r3.at[s], s2s.at[s], s2r.at[s], y_peer).wait_recv()
        pre = r2[s, yh] + r3[s]
        sigma = jax.nn.sigmoid(pre)
        diff = pre * sigma - tgt[s].astype(F32)
        up_at(s)[...] = (2.0 * diff * sigma * (1.0 + pre * (1.0 - sigma))).astype(BF16)
        err[...] += fold(diff * diff)
        copy(up_at(s), up_at(s), s3s.at[s], s3r.at[s], y_peer).start()

    def s4(s):
        copy(up_at(s), up_at(s), s3s.at[s], s3r.at[s], y_peer).wait_recv()
        src = up.at[s, aligned(x, blk), aligned(core, cols)]
        for o in range(1, NQ):
            x_, c_ = q_dev(o)
            copy(src, src, s4s.at[s], s4r.at[s], dev(x_, yh, yl, z, c_)).start()

    def seven(s):
        return up.at[s, pl.ds(0, (NQ - 1) * blk // NC)]

    def s5(s):
        copy(seven(s), seven(s), s4s.at[s], s4r.at[s], sib).wait_recv()
        u = up[s].T

        def cols_of(i, carry):
            at = aligned(i, 256 if kh % 256 == 0 else 128)
            gacc[:, at] += jnp.dot(u, xs[s, :, at], preferred_element_type=F32)
            return carry

        lax.fori_loop(0, kh // (256 if kh % 256 == 0 else 128), cols_of, 0)

    for j in range(NYL):
        y_ = rem(yl + j, NYL)
        if j == 0:
            local.wait()
            at = own_rows(yl, 1 - core)
            copy(xs.at[z, at], xs.at[z, at], ys, yr.at[yl, 1 - core], sib).wait_recv()
        else:
            for c_ in range(NC):
                at = own_rows(y_, c_)
                copy(xs.at[z, at], xs.at[z, at], ys, yr.at[y_, c_], sib).wait_recv()
        forward(z, y_, 0, True)
        forward(z, y_, 0, False)
    red_send(0, 1, red_recv(0, 0))
    local_w.wait()
    send_w.wait_recv()
    s1(z)
    red_send(0, 2, red_recv(0, 1))
    total = red_recv(0, 2)
    energy_v[...] = jnp.broadcast_to(jnp.sum(total, axis=(0, 1), keepdims=True), energy_v.shape)

    last = NZ // 2

    def each(d, fn):
        def go(i, carry):
            fn(rem(z + NZ + (2 * i - 1) * d, NZ))
            return carry

        lax.fori_loop(0, jnp.where(d == 0, 1, 2), go, 0)

    stages = (s2, s3, s4, s5)

    def step(d, carry):
        below, above = down_slab(d), up_slab(d)
        for j in range(NYL):
            y_ = rem(yl + j, NYL)
            wait_piece(below, y_)
            if j < NYL // 2:
                forward(below, y_, d, True)
            else:
                pl.when(d < last - 1)(functools.partial(forward, below, y_, d, True))
            wait_piece(above, y_)
            if j >= NYL // 2:
                forward(above, y_, d, False)
            else:
                pl.when(d < last - 1)(functools.partial(forward, above, y_, d, False))
            if j < len(stages):
                each(d - 1, stages[j])
        for stage in stages[NYL:]:
            each(d - 1, stage)
        each(d, s1)
        return carry

    lax.fori_loop(1, last, step, 0)

    far = up_slab(last)
    prev = last - 1
    for j in range(NYL // 2):
        wait_piece(far, rem(yl + j, NYL))
        wait_piece(far, rem(yl + j + NYL // 2, NYL))
        each(prev, stages[j])
    s1(far)
    for stage in stages[NYL // 2 :]:
        each(prev, stage)
    for stage in stages:
        stage(far)

    send_g = copy(gacc.at[aligned(1 - core, cols)], grecv, gs, gr, sib)
    send_g.start()
    factor = float(D * FW) / energy_v[0:1, 0:1]

    def finish(ref, first, h):
        def go(i, total):
            at = aligned(h * groups + i, GROUP)
            wgrad = ref[pl.ds(first, cols), aligned(i, GROUP)].T
            g = factor * (ss[at] * wgrad) + reg[at]
            grad[at] = g
            return total + fold(g * g)

        return functools.partial(lax.fori_loop, 0, groups, go)

    squares = finish(gacc, pl.multiple_of(core * cols, cols), core)(jnp.zeros((8, cols), F32))
    send_g.wait_recv()
    squares = finish(grecv, 0, 1 - core)(squares)

    row = lax.broadcasted_iota(jnp.int32, (8, cols), 0)
    parts = [jnp.sum(v, axis=0, keepdims=True) for v in (squares, err[...], regular)]
    tile = jnp.zeros((8, cols), F32)
    for i, v in enumerate(parts):
        tile = jnp.where(row == i, v, tile)
    red_send(1, 0, tile)
    red_send(1, 1, red_recv(1, 0))
    red_send(1, 2, red_recv(1, 1))
    sums = jnp.sum(red_recv(1, 2), axis=1, keepdims=True)
    rms = jnp.sqrt(sums[0:1] / float(D * FW) + EPSILON)
    inverse = STEP_SIZE / rms
    loss[...] = sums[1:2] / energy_v[0:1, 0:1] + REG_WEIGHT * sums[2:3] / float(D * FW)

    def result(g, carry):
        at = aligned(g, GROUP)
        round_v[at] = round_v[at] - grad[at] * inverse
        return carry

    lax.fori_loop(0, NC * groups, result, 0)
    store = pltpu.make_async_copy(round_v, out, out_sem)
    store.start()

    all_rows = xs.at[0, pl.ds(0, (2 * NYL - 1) * rows)]
    copy(all_rows, all_rows, ys, yr.at[0, 0], sib).wait_send()
    for k in range(2):
        for d in range(last):
            n = NYL * blk if d < last - 1 else NYL * blk // 2
            sent = xs.at[0, pl.ds(0, n)]
            copy(sent, sent, zs.at[k, d], zr.at[0, 0], z_up).wait_send()
    send_w.wait_send()
    send_g.wait_send()

    def sent_stages(s, carry):
        copy(rbuf.at[s], rbuf.at[s], s1s.at[s], s1r.at[s], sib).wait_send()
        copy(r3.at[s], r3.at[s], s2s.at[s], s2r.at[s], y_peer).wait_send()
        copy(up_at(s), up_at(s), s3s.at[s], s3r.at[s], y_peer).wait_send()
        copy(seven(s), seven(s), s4s.at[s], s4r.at[s], sib).wait_send()
        return carry

    lax.fori_loop(0, NZ, sent_stages, 0)
    for i in range(2):
        for st in range(3):
            red_done(i, st)
    store.wait()


def local(tokens, codes, expo, rounding, target):
    rows, kd = tokens.shape
    cols = codes.shape[1]
    kh = kd // NC
    blk = rows * NC
    half = blk // NYH
    slab = NYL * blk
    dma = pltpu.SemaphoreType.DMA
    vmem = pltpu.VMEM
    out, loss = pl.pallas_call(
        kernel,
        out_shape=(
            jax.ShapeDtypeStruct(rounding.shape, F32),
            jax.ShapeDtypeStruct((1, 1), F32),
        ),
        in_specs=[pl.BlockSpec(memory_space=pl.ANY)] * 5,
        out_specs=(pl.BlockSpec(memory_space=pl.ANY), pl.BlockSpec(memory_space=pltpu.VMEM)),
        scratch_shapes=[
            vmem((NZ, slab, kh), BF16),
            vmem((kd, cols), jnp.int32),
            vmem(expo.shape, jnp.int32),
            vmem((kd, cols), F32),
            vmem((NZ, half, cols), BF16),
            vmem(expo.shape, F32),
            vmem((kd, cols), F32),
            vmem((kd, cols), F32),
            vmem((kd, cols), F32),
            vmem((kd, cols), BF16),
            vmem((kh, NC * cols), BF16),
            vmem((NZ, slab, NC * cols), F32),
            vmem((NZ, NQ - 1, blk, cols), F32),
            vmem((NZ, NYH, half, cols), F32),
            vmem((NZ, half, cols), F32),
            vmem((NZ, slab, NC * cols), BF16),
            vmem((NC * cols, kh), F32),
            vmem((cols, kh), F32),
            vmem((8, cols), F32),
            vmem((2, 3, 8, cols), F32),
            vmem((2, 3, max(NQ, NY, NZ) - 1, 8, cols), F32),
            vmem((8, cols), F32),
            dma((3,)), dma, dma, dma, dma,
            dma, dma((NYL, NC)), dma((2, NZ // 2)), dma((NZ, NYL)), dma, dma,
            dma((NZ,)), dma((NZ,)), dma((NZ,)), dma((NZ,)), dma((NZ,)), dma((NZ,)), dma((NZ,)), dma((NZ,)),
            dma, dma, dma((2, 3)), dma((2, 3)),
        ],
        compiler_params=pltpu.CompilerParams(
            collective_id=0, has_side_effects=True, vmem_limit_bytes=48 * 1024 * 1024
        ),
    )(tokens, codes, expo, rounding, target)
    return out, loss.reshape(())


def solution(mesh):
    in_specs = (P("dp", "mp"), P("mp", "dp"), P("mp", "dp"), P("mp", "dp"), P(None, "dp"))
    out_specs = (P("mp", "dp"), P())
    return jax.shard_map(local, mesh=mesh, in_specs=in_specs, out_specs=out_specs, check_vma=False)
```

time: 542 us -> 185 us (0.34)
  waiting for transfers between devices: 259 us -> 0 us
  blocking collectives: 232 us -> 0 us
  Pallas kernels: 0 us -> 176 us
  matrix products: 19.7 us -> 0 us
  between operations: 19.2 us -> 2.34 us
    psum x2 -> x0, blocking collectives: 232 us -> none  [the longest x1 136 us: local(): energy = lax.psum(local_energy, 'dp')]
    pallas_call x0 -> x1, Pallas kernels: none -> 176 us  [local(): pl.pallas_call(kernel, out_shape=(jax.ShapeDtypeStruct(rounding.shape, F3...]
    all_gather x1 -> x0, waiting for transfers between devices: 136 us -> none  [local(): gathered = lax.all_gather(tokens, 'dp', axis=0, tiled=True)]
    psum x1 -> x0, waiting for transfers between devices: 122 us -> none  [local(): pre = lax.psum(partial_pre, 'mp')]
    dot_general x2 -> x0, matrix products: 19.7 us -> none  [the longest x1 10 us: local(): partial_pre = jnp.dot(gathered, weights, preferred_element_type=jnp.float32)]
  transfers between devices with their start and end apart: 2 -> 0, of which waited for: 2 -> 0; matrix products, arithmetic and copies ran while one was open for 1% -> 0% of each run, Pallas kernels for 0% -> 0%
where the time goes in v1:
time: 185 us; the launch traced here: 184 us
  Pallas kernels  176 us (95%)
  local copies, waits for them, and re-layouts  6.17 us (3%)
  between operations  2.34 us (1%)
    pallas_call x1, Pallas kernels, local(): pl.pallas_call(kernel, out_shape=(jax.ShapeDtypeStruct(rounding.shape, F3...  176 us
    unnamed x11, local copies, waits for them, and re-layouts  6.17 us

profile of v1, /device:TPU:1, one launch (start us, length us, event | category | flops | bytes accessed | tf_op | source)
XLA Modules:
  0.0 184.2 jit_solution(11068968379374800550)
XLA Ops:
  0.6 0.0 copy-start
  0.6 1.2 copy-done
  1.9 0.0 copy-start.1
  1.9 1.2 copy-done.1
  3.1 0.0 copy-start.2
  3.1 1.1 copy-done.2
  4.2 0.0 copy-start.3
  4.2 0.9 copy-done.3
  5.1 0.0 copy-start.4
  5.1 0.7 copy-done.4
  5.8 175.7 %shard_map.68 = (f32[2048,128]{1,0:T(8,128)S(1)}, f32[1,1]{1,0:T(1,128)}) custom-call(bf16[48,2048]{1,0:T(8,128)(2,1)S(1)} %copy-done.3, s32[2048,128]{1,0:T(8,128)S(1)} %copy-done, s32[16,128]{1,0:T(8,128)S(1)} %copy-done.4, f32[2048,128]{1,0:T(8,128)S(1)} %copy-done.1, bf16[3072,128]{1,0:T(8,128)(2,1)S(1)} %copy-done.2), custom_call_target="tpu_custom_call" | custom-call | tf_op jit(solution)/shard_map/pallas_call | solution.py:405
  181.5 1.0 copy.9
Async XLA Ops:
  0.6 1.2 copy-start
  1.9 1.2 copy-start.1
  3.1 1.1 copy-start.2
  4.2 0.9 copy-start.3
  5.1 0.7 copy-start.4

commit v2 on v1

v2 whole, which is shorter than its diff:
```python
import functools

import jax
import jax.numpy as jnp
from jax import lax
from jax.experimental import pallas as pl
from jax.experimental.pallas import tpu as pltpu
from jax.sharding import PartitionSpec as P

D = 16384
FW = 8192
GROUP = 128
STRETCH_HIGH = 1.1
STRETCH_LOW = -0.1
LIMIT = 2.3978952727983707
REG_WEIGHT = 0.01
STEP_SIZE = 0.5
EPSILON = 1e-06

NX, NYL, NYH, NZ, NC = 4, 4, 2, 8, 2
NQ = NX * NC
NY = NYL * NYH
B_COLS = 128

PLAN = (((1, 2),), (), ((2, 4), (1, 3)), ((3, 5), (0, 1)))
FAR = (((1, 2), (2, 4)), ())
TAIL = ((0, 1), (1, 3), (0, 2), (3, 5), (2, 5), (0, 3), (1, 4), (0, 4), (1, 5), (0, 5))
MESH = pl.DeviceIdType.MESH
F32 = jnp.float32
BF16 = jnp.bfloat16


def rem(a, n):
    return lax.rem(a, jnp.int32(n))


def div(a, n):
    return lax.div(a, jnp.int32(n))


def aligned(a, n):
    return pl.ds(pl.multiple_of(a * n, n), n)


def kernel(
    tokens, codes, expo, rounding, target, out, loss,
    xs, codes_v, expo_v, round_v, tgt, scale_v, ss, reg, grad, w_full, w, part, sbuf, rbuf, r2, r3, up, gacc, grecv,
    err, red_src, red_buf, energy_v,
    in_sem, tgt_sem, loc_sem, wl_sem, out_sem,
    ts, tr, bs, br, zf, za, zb, zr, ws, wr, s1s, s1r, s2s, s2r, s3s, s3r, s4s, s4r, gs, gr, rs, rr,
):
    dp, mp = lax.axis_index("dp"), lax.axis_index("mp")
    core = rem(dp, NC)
    z = rem(div(dp, NC), NZ)
    yl = div(dp, NC * NZ)
    x = rem(mp, NX)
    yh = div(mp, NX)
    q = x * NC + core
    y = yh * NYL + yl

    def dev(x_, yh_, yl_, z_, c_):
        return ((yl_ * NZ + z_) * NC + c_, yh_ * NX + x_)

    rows, kd = tokens.shape
    kh = kd // NC
    blk = rows * NC
    cols = codes.shape[1]
    groups = kh // GROUP
    a_cols = kh - B_COLS
    last = NZ // 2

    def q_dev(o):
        t = rem(q + o, NQ)
        return dev(div(t, NC), yh, yl, z, rem(t, NC))

    def y_dev(o):
        t = rem(y + o, NY)
        return dev(x, div(t, NYL), rem(t, NYL), z, core)

    def z_dev(o):
        return dev(x, yh, yl, rem(z + o, NZ), core)

    def x_dev(o):
        return dev(rem(x + o, NX), yh, yl, z, core)

    z_next = (z_dev(1), z_dev(NZ - 1))
    line_next = (dev(x, yh, rem(yl + 1, NYL), z, core), dev(x, yh, rem(yl + NYL - 1, NYL), z, core))
    has_next = (yl < NYL - 1, yl > 0)
    sib = dev(x, yh, yl, z, 1 - core)
    y_peer = dev(x, 1 - yh, yl, z, core)

    def copy(src, dst, ssem, rsem, to):
        return pltpu.make_async_remote_copy(
            src_ref=src, dst_ref=dst, send_sem=ssem, recv_sem=rsem, device_id=to, device_id_type=MESH
        )

    def same(ref, ssem, rsem, to):
        return copy(ref, ref, ssem, rsem, to)

    loads = [
        pltpu.make_async_copy(rounding, round_v, in_sem.at[0]),
        pltpu.make_async_copy(codes, codes_v, in_sem.at[1]),
        pltpu.make_async_copy(expo, expo_v, in_sem.at[2]),
    ]
    for load in loads:
        load.start()
    for s in range(NZ):
        at = pl.multiple_of(x * (NZ * blk) + s * blk, 16)
        pltpu.make_async_copy(target.at[pl.ds(at, blk)], tgt.at[s], tgt_sem).start()

    def token_half(h):
        return tokens.at[:, aligned(h, kh)]

    def own_rows(c_):
        return pl.ds(pl.multiple_of(yl * blk + c_ * rows, 16), rows)

    local = pltpu.make_async_copy(token_half(core), xs.at[z, own_rows(core)], loc_sem)
    local.start()

    barrier = pltpu.get_barrier_semaphore()
    partners = [q_dev(o) for o in range(1, NQ)] + [y_dev(o) for o in range(1, NY)] + [z_dev(o) for o in range(1, NZ)]
    for partner in partners:
        pl.semaphore_signal(barrier, inc=1, device_id=partner, device_id_type=MESH)
    pl.semaphore_wait(barrier, len(partners))

    send_t = copy(token_half(1 - core), xs.at[z, own_rows(core)], ts, tr, sib)
    send_t.start()

    def piece(s, y_):
        return xs.at[s, aligned(y_, blk)]

    def a_piece(s, y_):
        return xs.at[s, aligned(y_, blk), pl.ds(0, a_cols)]

    def b_piece(s, y_):
        return xs.at[s, aligned(y_, blk), pl.ds(a_cols, B_COLS)]

    def z_send(s, j, y_, d, k):
        if j == 0:
            same(piece(s, y_), zf.at[k, d], zr.at[s, y_], z_next[k]).start()
        else:
            same(a_piece(s, y_), za.at[k, d], zr.at[s, y_], z_next[k]).start()

    def z_wait(s, j, y_):
        same((a_piece if j else piece)(s, y_), zf.at[0, 0], zr.at[s, y_], sib).wait_recv()

    def line_send(s, y_, side, ref):
        @pl.when(has_next[side])
        def _():
            same(ref(s, y_), bs.at[side, s, y_], br.at[s, y_], line_next[side]).start()

    def line_pass(s, j, ref, then):
        for side in range(2):
            y_ = yl - j if side == 0 else yl + j

            @pl.when(y_ >= 0 if side == 0 else y_ < NYL)
            def _(side=side, y_=y_):
                same(ref(s, y_), bs.at[side, s, y_], br.at[s, y_], sib).wait_recv()
                line_send(s, y_, side, ref)
                then(y_)

    def red_send(i, st, value):
        red_src[i, st] = value
        for o in range(1, (NQ, NY, NZ)[st]):
            to = (q_dev, y_dev, z_dev)[st](o)
            copy(red_src.at[i, st], red_buf.at[i, st, o - 1], rs.at[i, st], rr.at[i, st], to).start()

    def red_got(i, st):
        n = (NQ, NY, NZ)[st] - 1
        return same(red_buf.at[i, st, pl.ds(0, n)], rs.at[i, st], rr.at[i, st], sib)

    def red_recv(i, st):
        red_got(i, st).wait_recv()
        total = red_src[i, st]
        for o in range((NQ, NY, NZ)[st] - 1):
            total += red_buf[i, st, o]
        return total

    def fold(a):
        return a.reshape(a.shape[0] // 8, 8, a.shape[1]).sum(axis=0)

    local.wait()
    send_t_back = copy(token_half(1 - core), xs.at[z, own_rows(1 - core)], ts, tr, sib)
    send_t_back.wait_recv()
    for k in range(2):
        z_send(z, 0, yl, 0, k)
        line_send(z, yl, k, piece)

    for load in loads:
        load.wait()
    scale_v[...] = jnp.exp2(expo_v[...].astype(F32)) * D ** (-0.5)

    def group_weights(g, total):
        at = aligned(g, GROUP)
        r = round_v[at]
        sigma = jax.nn.sigmoid(r)
        soft = jnp.clip(sigma * (STRETCH_HIGH - STRETCH_LOW) + STRETCH_LOW, 0.0, 1.0)
        slope = jnp.where(jnp.abs(r) < LIMIT, (STRETCH_HIGH - STRETCH_LOW) * sigma * (1.0 - sigma), 0.0)
        scale = scale_v[pl.ds(g, 1)]
        w_full[at] = (scale * (codes_v[at].astype(F32) + soft)).astype(BF16)
        centered = 2.0 * soft - 1.0
        cube = centered * centered * centered
        ss[at] = scale * slope
        reg[at] = -REG_WEIGHT * 8.0 * cube * slope
        return total + fold(1.0 - cube * centered)

    def half_rows(h):
        return aligned(h, kh)

    def weights(h, total):
        return lax.fori_loop(h * groups, (h + 1) * groups, group_weights, total)

    w_cols = w.at[:, aligned(core, cols)]
    regular = weights(1 - core, jnp.zeros((8, cols), F32))
    send_w = copy(w_full.at[half_rows(1 - core)], w_cols, ws, wr, sib)
    send_w.start()
    regular = weights(core, regular)
    local_w = pltpu.make_async_copy(w_full.at[half_rows(core)], w_cols, wl_sem)
    local_w.start()

    pltpu.make_async_copy(tgt, tgt, tgt_sem).wait()
    err[...] = jnp.zeros_like(err)
    energy = jnp.zeros((8, cols), F32)
    for s in range(NZ):
        t = tgt[s].astype(F32)
        energy += fold(t * t)
    red_send(0, 0, energy)
    gacc[...] = jnp.zeros_like(gacc)

    own_cols, sib_cols = aligned(core, cols), aligned(1 - core, cols)
    own_x = aligned(x, blk)

    def t1(s):
        def rows_of(j, carry):
            at = aligned(j, blk)
            part[s, at] = jnp.dot(xs[s, at], w[...], preferred_element_type=F32)
            return carry

        lax.fori_loop(0, NYL, rows_of, 0)
        copy(part.at[s, :, sib_cols], sbuf.at[s], s1s.at[s], s1r.at[s], sib).start()

    def t2(s):
        same(sbuf.at[s], s1s.at[s], s1r.at[s], sib).wait_recv()
        sbuf[s] = sbuf[s] + part[s, :, own_cols]
        for o in range(1, NX):
            src = sbuf.at[s, aligned(rem(x + o, NX), blk)]
            copy(src, rbuf.at[s, o - 1], s2s.at[s], s2r.at[s], x_dev(o)).start()

    def t3(s):
        same(rbuf.at[s], s2s.at[s], s2r.at[s], sib).wait_recv()
        total = sbuf[s, own_x]
        for o in range(NX - 1):
            total += rbuf[s, o]
        r2[s] = total
        copy(r2.at[s], r3.at[s], s3s.at[s], s3r.at[s], y_peer).start()

    def t4(s):
        same(r3.at[s], s3s.at[s], s3r.at[s], y_peer).wait_recv()
        pre = r2[s] + r3[s]
        sigma = jax.nn.sigmoid(pre)
        diff = pre * sigma - tgt[s].astype(F32)
        up[s, own_x, own_cols] = (2.0 * diff * sigma * (1.0 + pre * (1.0 - sigma))).astype(BF16)
        err[...] += fold(diff * diff)
        for o in range(1, NQ):
            same(up.at[s, own_x, own_cols], s4s.at[s], s4r.at[s], q_dev(o)).start()

    def seven(s):
        return same(up.at[s, pl.ds(0, (NQ - 1) * blk // NC)], s4s.at[s], s4r.at[s], sib)

    wide = min(kh, 256)

    def t5(s):
        seven(s).wait_recv()
        u = up[s].T

        def cols_of(i, carry):
            at = aligned(i, wide)
            gacc[:, at] += jnp.dot(u, xs[s, :, at], preferred_element_type=F32)
            return carry

        lax.fori_loop(0, kh // wide, cols_of, 0)

    def each(d, stage):
        def go(i, carry):
            (t1, t2, t3, t4, t5)[stage - 1](rem(z + NZ + (2 * i - 1) * d, NZ))
            return carry

        lax.fori_loop(0, jnp.where(d > 0, 2, jnp.where(d == 0, 1, 0)), go, 0)

    def at_far(back, stage):
        if back:
            each(jnp.int32(last - back), stage)
        else:
            (t1, t2, t3, t4, t5)[stage - 1](far)

    def energy_stage(st):
        if st < 3:
            red_send(0, st, red_recv(0, st - 1))
        else:
            total = red_recv(0, 2)
            energy_v[...] = jnp.broadcast_to(jnp.sum(total, axis=(0, 1), keepdims=True) * (1.0 / NYH), energy_v.shape)

    def none(y_):
        return None

    def tick(d, j):
        slabs = rem(z + NZ - d, NZ), rem(z + d, NZ)

        def take(rel, y_):
            for k in range(2):
                z_wait(slabs[k], rel, y_)
                if (rel < NYL // 2) == (k == 0):
                    z_send(slabs[k], rel, y_, d, k)
                else:
                    pl.when(d < last - 1)(functools.partial(z_send, slabs[k], rel, y_, d, k))

        if j == 0:
            take(0, yl)
            for s in slabs:
                for side in range(2):
                    line_send(s, yl, side, b_piece)
        else:
            pl.when(yl >= j)(functools.partial(take, NYL - j, yl - j))
            pl.when(yl + j < NYL)(functools.partial(take, j, yl + j))
            for s in slabs:
                line_pass(s, j, b_piece, none)
        if j == NYL - 1:

            @pl.when(d == last - 1)
            def _():
                for i in range(1, NYL):
                    k = 0 if i < NYL // 2 else 1
                    at = rem(yl + i, NYL)
                    same(b_piece(slabs[k], at), zb.at[k], br.at[slabs[k], at], z_next[k]).start()

    for j in range(1, NYL):

        def onward(y_):
            for k in range(2):
                z_send(z, 1, y_, 0, k)

        line_pass(z, j, piece, onward)
        tick(jnp.int32(1), j - 1)
    local_w.wait()
    send_w.wait_recv()
    t1(z)
    tick(jnp.int32(1), NYL - 1)
    energy_stage(1)
    t2(z)
    each(jnp.int32(1), 1)

    def step(d, carry):
        for j in range(NYL):
            tick(d, j)
            if j == 0:
                pl.when(d == 2)(functools.partial(t3, z))
            for back, stage in PLAN[j]:
                each(d - back, stage)
            if j == NYL - 1:
                for st in range(2, 4):
                    if st < last:
                        pl.when(d == st)(functools.partial(energy_stage, st))
        return carry

    lax.fori_loop(2, last, step, 0)

    far = rem(z + last, NZ)
    for j in range(NYL // 2):
        for jj in (j, j + NYL // 2):
            z_wait(far, jj, rem(yl + jj, NYL))
        for work in FAR[j]:
            at_far(*work)
    for j in range(1, NYL):
        at = rem(yl + j, NYL)
        same(b_piece(far, at), zb.at[0], br.at[far, at], sib).wait_recv()
    if last == 2:
        t3(z)
    for st in range(last, 4):
        energy_stage(st)
    for work in TAIL:
        at_far(*work)

    send_g = copy(gacc.at[sib_cols], grecv, gs, gr, sib)
    send_g.start()
    factor = float(D * FW) / energy_v[0:1, 0:1]

    def finish(ref, first, h):
        def go(i, total):
            at = aligned(h * groups + i, GROUP)
            wgrad = ref[pl.ds(first, cols), aligned(i, GROUP)].T
            g = factor * (ss[at] * wgrad) + reg[at]
            grad[at] = g
            return total + fold(g * g)

        return functools.partial(lax.fori_loop, 0, groups, go)

    squares = finish(gacc, pl.multiple_of(core * cols, cols), core)(jnp.zeros((8, cols), F32))
    send_g.wait_recv()
    squares = finish(grecv, 0, 1 - core)(squares)

    row = lax.broadcasted_iota(jnp.int32, (8, cols), 0)
    parts = [jnp.sum(v, axis=0, keepdims=True) for v in (squares, err[...] * (1.0 / NYH), regular)]
    tile = jnp.zeros((8, cols), F32)
    for i, v in enumerate(parts):
        tile = jnp.where(row == i, v, tile)
    red_send(1, 0, tile)
    red_send(1, 1, red_recv(1, 0))
    red_send(1, 2, red_recv(1, 1))
    sums = jnp.sum(red_recv(1, 2), axis=1, keepdims=True)
    rms = jnp.sqrt(sums[0:1] / float(D * FW) + EPSILON)
    inverse = STEP_SIZE / rms
    loss[...] = sums[1:2] / energy_v[0:1, 0:1] + REG_WEIGHT * sums[2:3] / float(D * FW)

    def result(g, carry):
        at = aligned(g, GROUP)
        round_v[at] = round_v[at] - grad[at] * inverse
        return carry

    lax.fori_loop(0, NC * groups, result, 0)
    store = pltpu.make_async_copy(round_v, out, out_sem)
    store.start()

    send_t.wait_send()
    for k in range(2):
        for d in range(last):
            n = NYL - 1
            if d < last - 1 or k == 0:
                same(piece(z, yl), zf.at[k, d], zr.at[z, yl], sib).wait_send()
            if d == last - 1:
                n = NYL // 2 - 1 if k == 0 else NYL - NYL // 2
                if n:
                    same(xs.at[z, pl.ds(0, n * blk), pl.ds(0, B_COLS)], zb.at[k], zr.at[z, yl], sib).wait_send()
            if n:
                same(xs.at[z, pl.ds(0, n * blk), pl.ds(0, a_cols)], za.at[k, d], zr.at[z, yl], sib).wait_send()

    def sent_line(s, ref):
        for side in range(2):
            for y_ in range(NYL):

                @pl.when(jnp.logical_and(has_next[side], y_ <= yl if side == 0 else y_ >= yl))
                def _(side=side, y_=y_):
                    same(ref(s, y_), bs.at[side, s, y_], br.at[s, y_], sib).wait_send()

    sent_line(z, piece)

    def sent_far_line(d, carry):
        for s in (rem(z + NZ - d, NZ), rem(z + d, NZ)):
            sent_line(s, b_piece)
        return carry

    lax.fori_loop(1, last, sent_far_line, 0)
    send_w.wait_send()
    send_g.wait_send()

    def sent_stages(s, carry):
        same(sbuf.at[s], s1s.at[s], s1r.at[s], sib).wait_send()
        same(rbuf.at[s], s2s.at[s], s2r.at[s], sib).wait_send()
        same(r3.at[s], s3s.at[s], s3r.at[s], y_peer).wait_send()
        seven(s).wait_send()
        return carry

    lax.fori_loop(0, NZ, sent_stages, 0)
    for i in range(2):
        for st in range(3):
            red_got(i, st).wait_send()
    store.wait()


def local(tokens, codes, expo, rounding, target):
    rows, kd = tokens.shape
    cols = codes.shape[1]
    kh = kd // NC
    blk = rows * NC
    slab = NYL * blk
    dma = pltpu.SemaphoreType.DMA
    vmem = pltpu.VMEM
    out, loss = pl.pallas_call(
        kernel,
        out_shape=(
            jax.ShapeDtypeStruct(rounding.shape, F32),
            jax.ShapeDtypeStruct((1, 1), F32),
        ),
        in_specs=[pl.BlockSpec(memory_space=pl.ANY)] * 5,
        out_specs=(pl.BlockSpec(memory_space=pl.ANY), pl.BlockSpec(memory_space=pltpu.VMEM)),
        scratch_shapes=[
            vmem((NZ, slab, kh), BF16),
            vmem((kd, cols), jnp.int32),
            vmem(expo.shape, jnp.int32),
            vmem((kd, cols), F32),
            vmem((NZ, blk, cols), BF16),
            vmem(expo.shape, F32),
            vmem((kd, cols), F32),
            vmem((kd, cols), F32),
            vmem((kd, cols), F32),
            vmem((kd, cols), BF16),
            vmem((kh, NC * cols), BF16),
            vmem((NZ, slab, NC * cols), F32),
            vmem((NZ, slab, cols), F32),
            vmem((NZ, NX - 1, blk, cols), F32),
            vmem((NZ, blk, cols), F32),
            vmem((NZ, blk, cols), F32),
            vmem((NZ, slab, NC * cols), BF16),
            vmem((NC * cols, kh), F32),
            vmem((cols, kh), F32),
            vmem((8, cols), F32),
            vmem((2, 3, 8, cols), F32),
            vmem((2, 3, max(NQ, NY, NZ) - 1, 8, cols), F32),
            vmem((8, cols), F32),
            dma((3,)), dma, dma, dma, dma,
            dma, dma, dma((2, NZ, NYL)), dma((NZ, NYL)), dma((2, NZ // 2)), dma((2, NZ // 2)), dma((2,)), dma((NZ, NYL)), dma, dma,
            dma((NZ,)), dma((NZ,)), dma((NZ,)), dma((NZ,)), dma((NZ,)), dma((NZ,)), dma((NZ,)), dma((NZ,)),
            dma, dma, dma((2, 3)), dma((2, 3)),
        ],
        compiler_params=pltpu.CompilerParams(
            collective_id=0, has_side_effects=True, vmem_limit_bytes=60 * 1024 * 1024
        ),
    )(tokens, codes, expo, rounding, target)
    return out, loss.reshape(())


def solution(mesh):
    in_specs = (P("dp", "mp"), P("mp", "dp"), P("mp", "dp"), P("mp", "dp"), P(None, "dp"))
    out_specs = (P("mp", "dp"), P())
    return jax.shard_map(local, mesh=mesh, in_specs=in_specs, out_specs=out_specs, check_vma=False)
```

time: 185 us -> 121 us (0.65)
  Pallas kernels: 176 us -> 117 us
  local copies, waits for them, and re-layouts: 6.17 us -> 2.26 us
    pallas_call x1, Pallas kernels: 176 us -> 117 us  [local(): pl.pallas_call(kernel, out_shape=(jax.ShapeDtypeStruct(rounding.shape, F3...]
    unnamed x11 -> x1, local copies, waits for them, and re-layouts: 6.17 us -> 2.26 us
where the time goes in v2:
time: 121 us
  Pallas kernels  117 us (97%)
  between operations  2.33 us (2%)
  local copies, waits for them, and re-layouts  2.26 us (2%)
    pallas_call x1, Pallas kernels, local(): pl.pallas_call(kernel, out_shape=(jax.ShapeDtypeStruct(rounding.shape, F3...  117 us

profile of v2, /device:TPU:1, one launch (start us, length us, event | category | flops | bytes accessed | tf_op | source)
XLA Modules:
  0.0 121.1 jit_solution(217053622460211488)
XLA Ops:
  0.6 116.5 %shard_map.68 = (f32[2048,128]{1,0:T(8,128)}, f32[1,1]{1,0:T(1,128)}) custom-call(bf16[48,2048]{1,0:T(8,128)(2,1)} %tokens.1, s32[2048,128]{1,0:T(8,128)} %codes.1, s32[16,128]{1,0:T(8,128)} %expo.1, f32[2048,128]{1,0:T(8,128)} %rounding.1, bf16[3072,128]{1,0:T(8,128)(2,1)} %target.1), custom_call_target="tpu_custom_call" | custom-call | tf_op jit(solution)/shard_map/pallas_call | solution.py:477
  117.2 2.3 %copy.9 = f32[2048,128]{1,0:T(8,128)} copy(f32[2048,128]{1,0:T(8,128)} %get-tuple-element.8) | data formatting | bytes 2097152

commit v3 on v2

--- a/solution.py
+++ b/solution.py
@@ -22,10 +22,18 @@
 NY = NYL * NYH
 B_COLS = 128
 
-PLAN = (((1, 2),), (), ((2, 4), (1, 3)), ((3, 5), (0, 1)))
-FAR = (((1, 2), (2, 4)), ())
-TAIL = ((0, 1), (1, 3), (0, 2), (3, 5), (2, 5), (0, 3), (1, 4), (0, 4), (1, 5), (0, 5))
+PLAN = (((1, 2),), ((3, 5),), ((1, 3),), ((2, 4), (0, 1)))
+BEFORE_FAR = ((1, 2),)
+FAR = (((2, 4), (3, 5)), ())
+TAIL = ((0, 1), (1, 3), (0, 2), (2, 5), (0, 3), (1, 4), (0, 4), (1, 5), (0, 5))
 MESH = pl.DeviceIdType.MESH
+
+
+def by_distance(n):
+    return sorted(range(1, n), key=lambda o: -min(o, n - o))
+
+
+VMEM_LIMIT = 60 << 20
 F32 = jnp.float32
 BF16 = jnp.bfloat16
 
@@ -43,11 +51,11 @@
 
 
 def kernel(
-    tokens, codes, expo, rounding, target, out, loss,
-    xs, codes_v, expo_v, round_v, tgt, scale_v, ss, reg, grad, w_full, w, part, sbuf, rbuf, r2, r3, up, gacc, grecv,
+    tokens, codes, expo, rounding, target, grad, inverse, loss,
+    xs, codes_v, expo_v, round_v, tgt, scale_v, ss, reg, ss_sib, reg_sib, grad_sib, w_full, w, part, sbuf, rbuf, r2, r3, up, gacc,
     err, red_src, red_buf, energy_v,
-    in_sem, tgt_sem, loc_sem, wl_sem, out_sem,
-    ts, tr, bs, br, zf, za, zb, zr, ws, wr, s1s, s1r, s2s, s2r, s3s, s3r, s4s, s4r, gs, gr, rs, rr,
+    in_sem, tgt_sem, loc_sem, wl_sem,
+    ts, tr, tz, tl, bs, bb, br, zf, za, zb, zr, ws, wr, fs, fr, s1s, s1r, s2s, s2r, s3s, s3r, s4s, s4r, gs, gr, rs, rr,
 ):
     dp, mp = lax.axis_index("dp"), lax.axis_index("mp")
     core = rem(dp, NC)
@@ -93,6 +101,9 @@
         return pltpu.make_async_remote_copy(
             src_ref=src, dst_ref=dst, send_sem=ssem, recv_sem=rsem, device_id=to, device_id_type=MESH
         )
+
+    def core_of(to, c_):
+        return (to[0] - core + c_, to[1])
 
     def same(ref, ssem, rsem, to):
         return copy(ref, ref, ssem, rsem, to)
@@ -119,12 +130,29 @@
 
     barrier = pltpu.get_barrier_semaphore()
     partners = [q_dev(o) for o in range(1, NQ)] + [y_dev(o) for o in range(1, NY)] + [z_dev(o) for o in range(1, NZ)]
+    partners += [core_of(to, 1 - core) for to in z_next + line_next]
     for partner in partners:
         pl.semaphore_signal(barrier, inc=1, device_id=partner, device_id_type=MESH)
     pl.semaphore_wait(barrier, len(partners))
 
-    send_t = copy(token_half(1 - core), xs.at[z, own_rows(core)], ts, tr, sib)
+    mine = xs.at[z, own_rows(core)]
+    for k, to in enumerate(z_next):
+        for h in range(NC):
+            copy(token_half(h), mine, zf.at[k, 0], tz.at[k, core], core_of(to, h)).start()
+    for side, to in enumerate(line_next):
+
+        @pl.when(has_next[side])
+        def _(side=side, to=to):
+            for h in range(NC):
+                copy(token_half(h), mine, bs.at[side, yl], tl.at[side, core], core_of(to, h)).start()
+
+    send_t = copy(token_half(1 - core), mine, ts, tr, sib)
     send_t.start()
+
+    def both_cores(s, y_, sems):
+        for c_ in range(NC):
+            at = pl.ds(pl.multiple_of(y_ * blk + c_ * rows, 16), rows)
+            same(xs.at[s, at], ts, sems.at[c_], sib).wait_recv()
 
     def piece(s, y_):
         return xs.at[s, aligned(y_, blk)]
@@ -134,6 +162,13 @@
 
     def b_piece(s, y_):
         return xs.at[s, aligned(y_, blk), pl.ds(a_cols, B_COLS)]
+
+    def place(p):
+        found = yl
+        for at in range(NYL):
+            order = sorted(range(NYL), key=lambda y_: (abs(y_ - at), y_))
+            found = jnp.where(yl == at, order[p], found)
+        return found
 
     def z_send(s, j, y_, d, k):
         if j == 0:
@@ -144,24 +179,27 @@
     def z_wait(s, j, y_):
         same((a_piece if j else piece)(s, y_), zf.at[0, 0], zr.at[s, y_], sib).wait_recv()
 
-    def line_send(s, y_, side, ref):
+    def line_send(y_, side):
         @pl.when(has_next[side])
         def _():
-            same(ref(s, y_), bs.at[side, s, y_], br.at[s, y_], line_next[side]).start()
-
-    def line_pass(s, j, ref, then):
+            same(piece(z, y_), bs.at[side, y_], br.at[z, y_], line_next[side]).start()
+
+    def line_pass(j, then):
         for side in range(2):
             y_ = yl - j if side == 0 else yl + j
 
             @pl.when(y_ >= 0 if side == 0 else y_ < NYL)
             def _(side=side, y_=y_):
-                same(ref(s, y_), bs.at[side, s, y_], br.at[s, y_], sib).wait_recv()
-                line_send(s, y_, side, ref)
+                if j == 1:
+                    both_cores(z, y_, tl.at[side])
+                else:
+                    same(piece(z, y_), bs.at[side, y_], br.at[z, y_], sib).wait_recv()
+                line_send(y_, side)
                 then(y_)
 
     def red_send(i, st, value):
         red_src[i, st] = value
-        for o in range(1, (NQ, NY, NZ)[st]):
+        for o in by_distance((NQ, NY, NZ)[st]):
             to = (q_dev, y_dev, z_dev)[st](o)
             copy(red_src.at[i, st], red_buf.at[i, st, o - 1], rs.at[i, st], rr.at[i, st], to).start()
 
@@ -178,13 +216,6 @@
 
     def fold(a):
         return a.reshape(a.shape[0] // 8, 8, a.shape[1]).sum(axis=0)
-
-    local.wait()
-    send_t_back = copy(token_half(1 - core), xs.at[z, own_rows(1 - core)], ts, tr, sib)
-    send_t_back.wait_recv()
-    for k in range(2):
-        z_send(z, 0, yl, 0, k)
-        line_send(z, yl, k, piece)
 
     for load in loads:
         load.wait()
@@ -214,6 +245,12 @@
     regular = weights(1 - core, jnp.zeros((8, cols), F32))
     send_w = copy(w_full.at[half_rows(1 - core)], w_cols, ws, wr, sib)
     send_w.start()
+    send_slopes = [
+        copy(ref.at[half_rows(1 - core)], other, fs.at[i], fr.at[i], sib)
+        for i, (ref, other) in enumerate(((ss, ss_sib), (reg, reg_sib)))
+    ]
+    for send in send_slopes:
+        send.start()
     regular = weights(core, regular)
     local_w = pltpu.make_async_copy(w_full.at[half_rows(core)], w_cols, wl_sem)
     local_w.start()
@@ -242,7 +279,7 @@
     def t2(s):
         same(sbuf.at[s], s1s.at[s], s1r.at[s], sib).wait_recv()
         sbuf[s] = sbuf[s] + part[s, :, own_cols]
-        for o in range(1, NX):
+        for o in by_distance(NX):
             src = sbuf.at[s, aligned(rem(x + o, NX), blk)]
             copy(src, rbuf.at[s, o - 1], s2s.at[s], s2r.at[s], x_dev(o)).start()
 
@@ -261,7 +298,7 @@
         diff = pre * sigma - tgt[s].astype(F32)
         up[s, own_x, own_cols] = (2.0 * diff * sigma * (1.0 + pre * (1.0 - sigma))).astype(BF16)
         err[...] += fold(diff * diff)
-        for o in range(1, NQ):
+        for o in by_distance(NQ):
             same(up.at[s, own_x, own_cols], s4s.at[s], s4r.at[s], q_dev(o)).start()
 
     def seven(s):
@@ -300,37 +337,34 @@
             total = red_recv(0, 2)
             energy_v[...] = jnp.broadcast_to(jnp.sum(total, axis=(0, 1), keepdims=True) * (1.0 / NYH), energy_v.shape)
 
-    def none(y_):
-        return None
-
-    def tick(d, j):
+    def tick(d, j, first=False):
         slabs = rem(z + NZ - d, NZ), rem(z + d, NZ)
-
-        def take(rel, y_):
-            for k in range(2):
-                z_wait(slabs[k], rel, y_)
-                if (rel < NYL // 2) == (k == 0):
-                    z_send(slabs[k], rel, y_, d, k)
-                else:
-                    pl.when(d < last - 1)(functools.partial(z_send, slabs[k], rel, y_, d, k))
-
+        y_ = place(j)
+        for k in range(2):
+            if first:
+                both_cores(slabs[k], y_, tz.at[k])
+            else:
+                z_wait(slabs[k], j, y_)
+            if (j < NYL // 2) == (k == 0):
+                z_send(slabs[k], j, y_, d, k)
+            else:
+                pl.when(d < last - 1)(functools.partial(z_send, slabs[k], j, y_, d, k))
         if j == 0:
-            take(0, yl)
             for s in slabs:
-                for side in range(2):
-                    line_send(s, yl, side, b_piece)
-        else:
-            pl.when(yl >= j)(functools.partial(take, NYL - j, yl - j))
-            pl.when(yl + j < NYL)(functools.partial(take, j, yl + j))
+                for o in range(1, NYL):
+                    to = dev(x, yh, rem(yl + o, NYL), z, core)
+                    same(b_piece(s, yl), bb.at[s, o], br.at[s, yl], to).start()
+        if j == NYL - 1:
             for s in slabs:
-                line_pass(s, j, b_piece, none)
-        if j == NYL - 1:
+                for o in range(1, NYL):
+                    at = rem(yl + o, NYL)
+                    same(b_piece(s, at), bb.at[s, o], br.at[s, at], sib).wait_recv()
 
             @pl.when(d == last - 1)
             def _():
                 for i in range(1, NYL):
                     k = 0 if i < NYL // 2 else 1
-                    at = rem(yl + i, NYL)
+                    at = place(i)
                     same(b_piece(slabs[k], at), zb.at[k], br.at[slabs[k], at], z_next[k]).start()
 
     for j in range(1, NYL):
@@ -339,15 +373,19 @@
             for k in range(2):
                 z_send(z, 1, y_, 0, k)
 
-        line_pass(z, j, piece, onward)
-        tick(jnp.int32(1), j - 1)
+        line_pass(j, onward)
+        tick(jnp.int32(1), j - 1, j == 1)
     local_w.wait()
     send_w.wait_recv()
+    local.wait()
+    copy(token_half(1 - core), xs.at[z, own_rows(1 - core)], ts, tr, sib).wait_recv()
     t1(z)
     tick(jnp.int32(1), NYL - 1)
     energy_stage(1)
     t2(z)
-    each(jnp.int32(1), 1)
+    for back, stage in PLAN[NYL - 1]:
+        if back == 0:
+            each(jnp.int32(1), stage)
 
     def step(d, carry):
         for j in range(NYL):
@@ -365,9 +403,11 @@
     lax.fori_loop(2, last, step, 0)
 
     far = rem(z + last, NZ)
+    for work in BEFORE_FAR:
+        at_far(*work)
     for j in range(NYL // 2):
         for jj in (j, j + NYL // 2):
-            z_wait(far, jj, rem(yl + jj, NYL))
+            z_wait(far, jj, place(jj))
         for work in FAR[j]:
             at_far(*work)
     for j in range(1, NYL):
@@ -380,23 +420,24 @@
     for work in TAIL:
         at_far(*work)
 
-    send_g = copy(gacc.at[sib_cols], grecv, gs, gr, sib)
+    factor = float(D * FW) / energy_v[0:1, 0:1]
+    for send in send_slopes:
+        send.wait_recv()
+
+    def finish(first, slopes, reg_ref, into, base):
+        def go(i, total):
+            at = aligned(base + i, GROUP)
+            g = factor * (slopes[at] * gacc[pl.ds(first, cols), aligned(i, GROUP)].T) + reg_ref[at]
+            into[at] = g
+            return total + fold(g * g)
+
+        return functools.partial(lax.fori_loop, 0, groups, go)
+
+    sib_first, own_first = (pl.multiple_of(c_ * cols, cols) for c_ in (1 - core, core))
+    squares = finish(sib_first, ss_sib, reg_sib, grad_sib, 0)(jnp.zeros((8, cols), F32))
+    send_g = copy(grad_sib, grad.at[half_rows(core)], gs, gr, sib)
     send_g.start()
-    factor = float(D * FW) / energy_v[0:1, 0:1]
-
-    def finish(ref, first, h):
-        def go(i, total):
-            at = aligned(h * groups + i, GROUP)
-            wgrad = ref[pl.ds(first, cols), aligned(i, GROUP)].T
-            g = factor * (ss[at] * wgrad) + reg[at]
-            grad[at] = g
-            return total + fold(g * g)
-
-        return functools.partial(lax.fori_loop, 0, groups, go)
-
-    squares = finish(gacc, pl.multiple_of(core * cols, cols), core)(jnp.zeros((8, cols), F32))
-    send_g.wait_recv()
-    squares = finish(grecv, 0, 1 - core)(squares)
+    squares = finish(own_first, ss, reg, grad, core * groups)(squares)
 
     row = lax.broadcasted_iota(jnp.int32, (8, cols), 0)
     parts = [jnp.sum(v, axis=0, keepdims=True) for v in (squares, err[...] * (1.0 / NYH), regular)]
@@ -404,21 +445,13 @@
     for i, v in enumerate(parts):
         tile = jnp.where(row == i, v, tile)
     red_send(1, 0, tile)
+    send_g.wait_recv()
     red_send(1, 1, red_recv(1, 0))
     red_send(1, 2, red_recv(1, 1))
     sums = jnp.sum(red_recv(1, 2), axis=1, keepdims=True)
     rms = jnp.sqrt(sums[0:1] / float(D * FW) + EPSILON)
-    inverse = STEP_SIZE / rms
+    inverse[...] = STEP_SIZE / rms
     loss[...] = sums[1:2] / energy_v[0:1, 0:1] + REG_WEIGHT * sums[2:3] / float(D * FW)
-
-    def result(g, carry):
-        at = aligned(g, GROUP)
-        round_v[at] = round_v[at] - grad[at] * inverse
-        return carry
-
-    lax.fori_loop(0, NC * groups, result, 0)
-    store = pltpu.make_async_copy(round_v, out, out_sem)
-    store.start()
 
     send_t.wait_send()
     for k in range(2):
@@ -433,24 +466,24 @@
             if n:
                 same(xs.at[z, pl.ds(0, n * blk), pl.ds(0, a_cols)], za.at[k, d], zr.at[z, yl], sib).wait_send()
 
-    def sent_line(s, ref):
-        for side in range(2):
-            for y_ in range(NYL):
-
-                @pl.when(jnp.logical_and(has_next[side], y_ <= yl if side == 0 else y_ >= yl))
-                def _(side=side, y_=y_):
-                    same(ref(s, y_), bs.at[side, s, y_], br.at[s, y_], sib).wait_send()
-
-    sent_line(z, piece)
+    for side in range(2):
+        for y_ in range(NYL):
+
+            @pl.when(jnp.logical_and(has_next[side], y_ <= yl if side == 0 else y_ >= yl))
+            def _(side=side, y_=y_):
+                same(piece(z, y_), bs.at[side, y_], br.at[z, y_], sib).wait_send()
 
     def sent_far_line(d, carry):
         for s in (rem(z + NZ - d, NZ), rem(z + d, NZ)):
-            sent_line(s, b_piece)
+            for o in range(1, NYL):
+                same(b_piece(s, yl), bb.at[s, o], br.at[s, yl], sib).wait_send()
         return carry
 
     lax.fori_loop(1, last, sent_far_line, 0)
     send_w.wait_send()
     send_g.wait_send()
+    for send in send_slopes:
+        send.wait_send()
 
     def sent_stages(s, carry):
         same(sbuf.at[s], s1s.at[s], s1r.at[s], sib).wait_send()
@@ -463,7 +496,6 @@
     for i in range(2):
         for st in range(3):
             red_got(i, st).wait_send()
-    store.wait()
 
 
 def local(tokens, codes, expo, rounding, target):
@@ -474,14 +506,15 @@
     slab = NYL * blk
     dma = pltpu.SemaphoreType.DMA
     vmem = pltpu.VMEM
-    out, loss = pl.pallas_call(
+    grad, inverse, loss = pl.pallas_call(
         kernel,
         out_shape=(
             jax.ShapeDtypeStruct(rounding.shape, F32),
             jax.ShapeDtypeStruct((1, 1), F32),
+            jax.ShapeDtypeStruct((1, 1), F32),
         ),
         in_specs=[pl.BlockSpec(memory_space=pl.ANY)] * 5,
-        out_specs=(pl.BlockSpec(memory_space=pl.ANY), pl.BlockSpec(memory_space=pltpu.VMEM)),
+        out_specs=(pl.BlockSpec(memory_space=pltpu.VMEM),) * 3,
         scratch_shapes=[
             vmem((NZ, slab, kh), BF16),
             vmem((kd, cols), jnp.int32),
@@ -491,7 +524,9 @@
             vmem(expo.shape, F32),
             vmem((kd, cols), F32),
             vmem((kd, cols), F32),
-            vmem((kd, cols), F32),
+            vmem((kh, cols), F32),
+            vmem((kh, cols), F32),
+            vmem((kh, cols), F32),
             vmem((kd, cols), BF16),
             vmem((kh, NC * cols), BF16),
             vmem((NZ, slab, NC * cols), F32),
@@ -501,21 +536,20 @@
             vmem((NZ, blk, cols), F32),
             vmem((NZ, slab, NC * cols), BF16),
             vmem((NC * cols, kh), F32),
-            vmem((cols, kh), F32),
             vmem((8, cols), F32),
             vmem((2, 3, 8, cols), F32),
             vmem((2, 3, max(NQ, NY, NZ) - 1, 8, cols), F32),
             vmem((8, cols), F32),
-            dma((3,)), dma, dma, dma, dma,
-            dma, dma, dma((2, NZ, NYL)), dma((NZ, NYL)), dma((2, NZ // 2)), dma((2, NZ // 2)), dma((2,)), dma((NZ, NYL)), dma, dma,
-            dma((NZ,)), dma((NZ,)), dma((NZ,)), dma((NZ,)), dma((NZ,)), dma((NZ,)), dma((NZ,)), dma((NZ,)),
+            dma((3,)), dma, dma, dma,
+            dma, dma, dma((2, NC)), dma((2, NC)), dma((2, NYL)), dma((NZ, NYL)), dma((NZ, NYL)), dma((2, NZ // 2)), dma((2, NZ // 2)), dma((2,)), dma((NZ, NYL)), dma, dma,
+            dma((2,)), dma((2,)), dma((NZ,)), dma((NZ,)), dma((NZ,)), dma((NZ,)), dma((NZ,)), dma((NZ,)), dma((NZ,)), dma((NZ,)),
             dma, dma, dma((2, 3)), dma((2, 3)),
         ],
         compiler_params=pltpu.CompilerParams(
-            collective_id=0, has_side_effects=True, vmem_limit_bytes=60 * 1024 * 1024
+            collective_id=0, has_side_effects=True, vmem_limit_bytes=VMEM_LIMIT
         ),
     )(tokens, codes, expo, rounding, target)
-    return out, loss.reshape(())
+    return rounding - grad * inverse, loss.reshape(())
 
 
 def solution(mesh):

time: 121 us -> 115 us (0.950)
  Pallas kernels: 117 us -> 109 us
  other arithmetic: 0 us -> 2.93 us
  local copies, waits for them, and re-layouts: 2.26 us -> 0.01 us
    pallas_call x1, Pallas kernels: 117 us -> 109 us  [local(): pl.pallas_call(kernel, out_shape=(jax.ShapeDtypeStruct(rounding.shape, F3...]
    sub x0 -> x1, other arithmetic: none -> 2.93 us  [local(): return (rounding - grad * inverse, loss.reshape(()))]
    unnamed x1 -> x2, local copies, waits for them, and re-layouts: 2.26 us -> 0.01 us
where the time goes in v3:
time: 115 us
  Pallas kernels  109 us (95%)
  other arithmetic  2.93 us (3%)
  between operations  2.42 us (2%)
    pallas_call x1, Pallas kernels, local(): pl.pallas_call(kernel, out_shape=(jax.ShapeDtypeStruct(rounding.shape, F3...  109 us
    sub x1, other arithmetic, local(): return (rounding - grad * inverse, loss.reshape(()))  2.93 us

profile of v3, /device:TPU:1, one launch (start us, length us, event | category | flops | bytes accessed | tf_op | source)
XLA Modules:
  0.0 114.6 jit_solution(15768657511947591828)
XLA Ops:
  0.6 0.0 copy-start
  0.6 109.2 %shard_map.68 = (f32[2048,128]{1,0:T(8,128)}, f32[1,1]{1,0:T(1,128)}, f32[1,1]{1,0:T(1,128)}) custom-call(bf16[48,2048]{1,0:T(8,128)(2,1)} %tokens.1, s32[2048,128]{1,0:T(8,128)} %codes.1, s32[16,128]{1,0:T(8,128)} %expo.1, f32[2048,128]{1,0:T(8,128)} %rounding.1, bf16[3072,128]{1,0:T(8,128)(2,1)} %target.1), custom_call_target="tpu_custom_call" | custom-call | tf_op jit(solution)/shard_map/pallas_call | solution.py:509
  109.9 0.0 copy-done
  109.9 2.9 %multiply_subtract_fusion = f32[2048,128]{1,0:T(8,128)} fusion(f32[2048,128]{1,0:T(8,128)S(1)} %copy-done, f32[2048,128]{1,0:T(8,128)} %get-tuple-element.5, f32[]{:T(128)} %bitcast), kind=kLoop, calls=%fused_computation | loop fusion | flops 524288 | bytes 3145732 | tf_op jit(solution)/shard_map/sub | solution.py:552
Async XLA Ops:
  0.6 109.3 %copy-start = (f32[2048,128]{1,0:T(8,128)S(1)}, f32[2048,128]{1,0:T(8,128)}, u32[]{:S(2)}) copy-start(f32[2048,128]{1,0:T(8,128)} %rounding.1) | copy-start | bytes 3145732

commit v4 on v3

--- a/solution.py
+++ b/solution.py
@@ -108,6 +108,11 @@
     def same(ref, ssem, rsem, to):
         return copy(ref, ref, ssem, rsem, to)
 
+    barrier = pltpu.get_barrier_semaphore()
+    partners = [y_dev(o) for o in by_distance(NY)] + [z_dev(o) for o in by_distance(NZ)] + [q_dev(o) for o in by_distance(NQ)]
+    partners += [core_of(to, 1 - core) for to in z_next + line_next]
+    for partner in partners:
+        pl.semaphore_signal(barrier, inc=1, device_id=partner, device_id_type=MESH)
     loads = [
         pltpu.make_async_copy(rounding, round_v, in_sem.at[0]),
         pltpu.make_async_copy(codes, codes_v, in_sem.at[1]),
@@ -128,11 +133,6 @@
     local = pltpu.make_async_copy(token_half(core), xs.at[z, own_rows(core)], loc_sem)
     local.start()
 
-    barrier = pltpu.get_barrier_semaphore()
-    partners = [q_dev(o) for o in range(1, NQ)] + [y_dev(o) for o in range(1, NY)] + [z_dev(o) for o in range(1, NZ)]
-    partners += [core_of(to, 1 - core) for to in z_next + line_next]
-    for partner in partners:
-        pl.semaphore_signal(barrier, inc=1, device_id=partner, device_id_type=MESH)
     pl.semaphore_wait(barrier, len(partners))
 
     mine = xs.at[z, own_rows(core)]
@@ -273,7 +273,7 @@
             part[s, at] = jnp.dot(xs[s, at], w[...], preferred_element_type=F32)
             return carry
 
-        lax.fori_loop(0, NYL, rows_of, 0)
+        lax.fori_loop(0, NYL, rows_of, 0, unroll=True)
         copy(part.at[s, :, sib_cols], sbuf.at[s], s1s.at[s], s1r.at[s], sib).start()
 
     def t2(s):
@@ -297,9 +297,9 @@
         sigma = jax.nn.sigmoid(pre)
         diff = pre * sigma - tgt[s].astype(F32)
         up[s, own_x, own_cols] = (2.0 * diff * sigma * (1.0 + pre * (1.0 - sigma))).astype(BF16)
-        err[...] += fold(diff * diff)
         for o in by_distance(NQ):
             same(up.at[s, own_x, own_cols], s4s.at[s], s4r.at[s], q_dev(o)).start()
+        err[...] += fold(diff * diff)
 
     def seven(s):
         return same(up.at[s, pl.ds(0, (NQ - 1) * blk // NC)], s4s.at[s], s4r.at[s], sib)
@@ -315,7 +315,7 @@
             gacc[:, at] += jnp.dot(u, xs[s, :, at], preferred_element_type=F32)
             return carry
 
-        lax.fori_loop(0, kh // wide, cols_of, 0)
+        lax.fori_loop(0, kh // wide, cols_of, 0, unroll=True)
 
     def each(d, stage):
         def go(i, carry):
@@ -431,7 +431,7 @@
             into[at] = g
             return total + fold(g * g)
 
-        return functools.partial(lax.fori_loop, 0, groups, go)
+        return functools.partial(lax.fori_loop, 0, groups, go, unroll=True)
 
     sib_first, own_first = (pl.multiple_of(c_ * cols, cols) for c_ in (1 - core, core))
     squares = finish(sib_first, ss_sib, reg_sib, grad_sib, 0)(jnp.zeros((8, cols), F32))

time: 115 us -> 113 us (0.983)
  Pallas kernels: 109 us -> 107 us
    pallas_call x1, Pallas kernels: 109 us -> 107 us  [local(): pl.pallas_call(kernel, out_shape=(jax.ShapeDtypeStruct(rounding.shape, F3...]
where the time goes in v4:
time: 113 us; the launch traced here: 112 us
  Pallas kernels  107 us (95%)
  other arithmetic  2.93 us (3%)
  between operations  2.42 us (2%)
    pallas_call x1, Pallas kernels, local(): pl.pallas_call(kernel, out_shape=(jax.ShapeDtypeStruct(rounding.shape, F3...  107 us
    sub x1, other arithmetic, local(): return (rounding - grad * inverse, loss.reshape(()))  2.93 us

profile of v4, /device:TPU:1, one launch (start us, length us, event | category | flops | bytes accessed | tf_op | source)
XLA Modules:
  0.0 112.1 jit_solution(17852239522581853021)
XLA Ops:
  0.6 0.0 copy-start
  0.6 106.7 %shard_map.68 = (f32[2048,128]{1,0:T(8,128)}, f32[1,1]{1,0:T(1,128)}, f32[1,1]{1,0:T(1,128)}) custom-call(bf16[48,2048]{1,0:T(8,128)(2,1)} %tokens.1, s32[2048,128]{1,0:T(8,128)} %codes.1, s32[16,128]{1,0:T(8,128)} %expo.1, f32[2048,128]{1,0:T(8,128)} %rounding.1, bf16[3072,128]{1,0:T(8,128)(2,1)} %target.1), custom_call_target="tpu_custom_call" | custom-call | tf_op jit(solution)/shard_map/pallas_call | solution.py:509
  107.4 0.0 copy-done
  107.4 2.9 %multiply_subtract_fusion = f32[2048,128]{1,0:T(8,128)} fusion(f32[2048,128]{1,0:T(8,128)S(1)} %copy-done, f32[2048,128]{1,0:T(8,128)} %get-tuple-element.5, f32[]{:T(128)} %bitcast), kind=kLoop, calls=%fused_computation | loop fusion | flops 524288 | bytes 3145732 | tf_op jit(solution)/shard_map/sub | solution.py:552
Async XLA Ops:
  0.6 106.7 %copy-start = (f32[2048,128]{1,0:T(8,128)S(1)}, f32[2048,128]{1,0:T(8,128)}, u32[]{:S(2)}) copy-start(f32[2048,128]{1,0:T(8,128)} %rounding.1) | copy-start | bytes 3145732

commit v5 on v4

--- a/solution.py
+++ b/solution.py
@@ -239,7 +239,7 @@
         return aligned(h, kh)
 
     def weights(h, total):
-        return lax.fori_loop(h * groups, (h + 1) * groups, group_weights, total)
+        return lax.fori_loop(0, groups, lambda i, t: group_weights(h * groups + i, t), total, unroll=2)
 
     w_cols = w.at[:, aligned(core, cols)]
     regular = weights(1 - core, jnp.zeros((8, cols), F32))

time: 113 us -> 113 us (level)
  no operation moved by 1% of the time
where the time goes in v5:
time: 113 us; the launch traced here: 112 us
  Pallas kernels  107 us (95%)
  other arithmetic  2.93 us (3%)
  between operations  2.42 us (2%)
    pallas_call x1, Pallas kernels, local(): pl.pallas_call(kernel, out_shape=(jax.ShapeDtypeStruct(rounding.shape, F3...  107 us
    sub x1, other arithmetic, local(): return (rounding - grad * inverse, loss.reshape(()))  2.93 us

profile of v5, /device:TPU:1, one launch (start us, length us, event | category | flops | bytes accessed | tf_op | source)
XLA Modules:
  0.0 112.1 jit_solution(17416649186250986299)
XLA Ops:
  0.6 0.0 copy-start
  0.6 106.7 %shard_map.68 = (f32[2048,128]{1,0:T(8,128)}, f32[1,1]{1,0:T(1,128)}, f32[1,1]{1,0:T(1,128)}) custom-call(bf16[48,2048]{1,0:T(8,128)(2,1)} %tokens.1, s32[2048,128]{1,0:T(8,128)} %codes.1, s32[16,128]{1,0:T(8,128)} %expo.1, f32[2048,128]{1,0:T(8,128)} %rounding.1, bf16[3072,128]{1,0:T(8,128)(2,1)} %target.1), custom_call_target="tpu_custom_call" | custom-call | tf_op jit(solution)/shard_map/pallas_call | solution.py:509
  107.4 0.0 copy-done
  107.4 2.9 %multiply_subtract_fusion = f32[2048,128]{1,0:T(8,128)} fusion(f32[2048,128]{1,0:T(8,128)S(1)} %copy-done, f32[2048,128]{1,0:T(8,128)} %get-tuple-element.5, f32[]{:T(128)} %bitcast), kind=kLoop, calls=%fused_computation | loop fusion | flops 524288 | bytes 3145732 | tf_op jit(solution)/shard_map/sub | solution.py:552
Async XLA Ops:
  0.6 106.7 %copy-start = (f32[2048,128]{1,0:T(8,128)S(1)}, f32[2048,128]{1,0:T(8,128)}, u32[]{:S(2)}) copy-start(f32[2048,128]{1,0:T(8,128)} %rounding.1) | copy-start | bytes 3145732
